TPU v7x, 128 devices: a whole 4x4x4 slice. The times are simulated.
128 devices in a mesh: terms: 8 (over y, core), blocks: 16 (over z, x).
Axes of the slice: x: 4, y: 4, z: 4, core: 2. Of those that a mesh axis runs over, the one named last changes fastest.
Arguments:
- psi: bfloat16 [2, 4096, 4096], P(None, 'blocks'), may hold values from -6 to 6
- shifts: int32 [48], P('terms'), may hold values from 0 to 15, as said below
- left_ops: bfloat16 [48, 16, 256, 256], P('terms'), may hold values from -0.0546875 to 0.0546875
- right_ops: bfloat16 [48, 16, 256, 256], P('terms'), may hold values from -0.375 to 0.375
Outputs:
- sigma: float32 [2, 4096, 4096], P(None, 'terms', 'blocks')
Inputs may be any that keep to these rules, and one draw needn't show every extreme that they name: Term t takes block (i, j + shifts[t]) to block (i + shifts[t], j), sectors counted modulo 16.
All inputs are finite; a program needn't handle non-finite values.
Results may differ from a plain program's by a relative error of at most 0.0029.
Values may be sent and summed in bfloat16 or wider, within the bound.
A program may use at most 256 MiB of HBM per device.

v0:
```python
import jax
import jax.numpy as jnp
from jax import lax
from jax.sharding import PartitionSpec as P


def first_section(vectors, shifts, right_ops):
    member_count, row_count, full_width = vectors.shape
    sector_count = right_ops.shape[1]
    width = right_ops.shape[2]
    blocked = vectors.reshape(member_count, row_count, sector_count, width)
    product = jnp.einsum(
        "vrnb,tnbc->vtrnc", blocked, right_ops, preferred_element_type=jnp.float32
    ).astype(jnp.bfloat16)
    positions = (
        jnp.arange(sector_count, dtype=jnp.int32)[None, :] + shifts[:, None]
    ) % sector_count
    shifted = jnp.take_along_axis(product, positions[None, :, None, :, None], axis=3)
    return shifted.reshape(member_count, shifts.shape[0], row_count, full_width)


def second_section(arrived, shifts, left_ops):
    member_count, term_count, full_rows, col_count = arrived.shape
    sector_count = left_ops.shape[1]
    width = left_ops.shape[2]
    blocked = arrived.reshape(member_count, term_count, sector_count, width, col_count)
    positions = (
        jnp.arange(sector_count, dtype=jnp.int32)[None, :] - shifts[:, None]
    ) % sector_count
    moved_blocks = jnp.take_along_axis(blocked, positions[None, :, :, None, None], axis=2)
    moved_left = jnp.take_along_axis(left_ops, positions[:, :, None, None], axis=1)
    partial_value = jnp.einsum(
        "tnab,vtnbc->vnac", moved_left, moved_blocks, preferred_element_type=jnp.float32
    )
    return partial_value.reshape(member_count, full_rows, col_count)


def per_device(psi, shifts, left_ops, right_ops):
    member_count = psi.shape[0]
    pieces = []
    for member in range(member_count):
        outgoing = first_section(psi[member : member + 1], shifts, right_ops)
        arrived = lax.all_to_all(outgoing, "blocks", split_axis=3, concat_axis=2, tiled=True)
        pieces.append(second_section(arrived, shifts, left_ops))
    partial_value = jnp.concatenate(pieces, axis=0)
    totals = lax.psum(partial_value, "terms")
    row_share = totals.shape[1] // lax.axis_size("terms")
    return lax.dynamic_slice_in_dim(totals, lax.axis_index("terms") * row_share, row_share, 1)


def solution(mesh):
    in_specs = (
        P(None, "blocks", None),
        P("terms"),
        P("terms", None, None, None),
        P("terms", None, None, None),
    )
    out_specs = P(None, "terms", "blocks")
    return jax.shard_map(
        per_device, mesh=mesh, in_specs=in_specs, out_specs=out_specs, check_vma=False
    )
```

profile of v0, /device:TPU:0, one launch (start us, length us, event | category | flops | bytes accessed | tf_op | source)
XLA Modules:
  0.0 783.5 jit_solution(10988035889899996627)
XLA Ops:
  6.5 0.7 clamp_shift-left_fusion.2
  7.3 0.7 and_bitcast_fusion.2
  8.0 3.9 fusion.34
  12.0 4.1 copy.62
  16.0 0.1 reshape.375
  16.1 2.5 copy.61
  18.6 0.0 copy-start.1
  18.6 10.2 %convert_bitcast_fusion = bf16[6,256,16,256]{1,3,0,2:T(8,128)(2,1)} fusion(bf16[256,16,256,1]{0,2,3,1:T(8,128)(2,1)} %bitcast.88, bf16[6,16,256,256]{3,2,1,0:T(8,128)(2,1)} %param.13), kind=kOutput, calls=%fused_computation.11 | convolution fusion | flops 3227516928 | bytes 27262976 | tf_op jit(solution)/shard_map/vrnb,tnbc->vtrnc/dot_general | solution.py:12
  28.7 0.0 copy-done.1
  28.7 9.8 %convert_bitcast_fusion.1 = bf16[6,256,16,256]{1,3,0,2:T(8,128)(2,1)} fusion(bf16[256,16,256,1]{0,2,3,1:T(8,128)(2,1)S(1)} %bitcast.89, bf16[6,16,256,256]{3,2,1,0:T(8,128)(2,1)} %param.13), kind=kOutput, calls=%fused_computation.12 | convolution fusion | flops 3227516928 | bytes 27262976 | tf_op jit(solution)/shard_map/vrnb,tnbc->vtrnc/dot_general | solution.py:12
  38.5 11.7 %gather_fusion.3 = bf16[96,256,256]{1,2,0:T(8,128)(2,1)} fusion(bf16[6,256,16,256]{1,3,0,2:T(8,128)(2,1)} %convert_bitcast_fusion, s32[96]{0:T(128)S(1)} %reshape.375), kind=kCustom, calls=%fused_computation.3.clone | custom fusion | bytes 25166592 | tf_op jit(solution)/shard_map/jit(take_along_axis)/gather | solution.py:18
  50.2 11.8 %gather_fusion = bf16[96,256,256]{1,2,0:T(8,128)(2,1)} fusion(bf16[6,256,16,256]{1,3,0,2:T(8,128)(2,1)} %convert_bitcast_fusion.1, s32[96]{0:T(128)S(1)} %reshape.375), kind=kCustom, calls=%fused_computation.clone | custom fusion | bytes 25166592 | tf_op jit(solution)/shard_map/jit(take_along_axis)/gather | solution.py:18
  62.0 13.7 %broadcast_select_fusion.2 = (bf16[1,6,256,16,256]{2,4,3,1,0:T(8,128)(2,1)S(1)}, bf16[1,6,256,16,256]{2,4,3,1,0:T(8,128)(2,1)}) fusion(bf16[1,6,256,16,256]{2,4,3,1,0:T(8,128)(2,1)} %bitcast.81, pred[6,16]{1,0:T(8,128)(4,1)S(1)} %and_bitcast_fusion.2, bf16[1,6,256,16,256]{2,4,3,1,0:T(8,128)(2,1)} %bitcast.80), kind=kLoop, calls=%fused_computation.17 | loop fusion | flops 12582912 | bytes 50331744 | tf_op jit(solution)/shard_map/jit(take_along_axis)/select_n | solution.py:18
  75.7 11.2 %copy.38 = bf16[1,6,256,16,256]{2,1,4,3,0:T(8,128)(2,1)} copy(bf16[1,6,256,16,256]{2,4,3,1,0:T(8,128)(2,1)S(1)} %get-tuple-element.10) | data formatting | bytes 25165824 | tf_op jit(solution)/shard_map/jit(take_along_axis)/select_n | solution.py:18
  86.8 8.0 %all-to-all-start = ((bf16[1,6,256,4096]{2,1,0,3:T(8,128)(2,1)}), bf16[1,6,256,4096]{2,1,0,3:T(8,128)(2,1)}, u32[]{:S(2)}, u32[]{:S(2)}) async-start(bf16[1,6,256,4096]{2,1,0,3:T(8,128)(2,1)} %bitcast.77), calls=%async_computation | async-start | bytes 33554432 | tf_op jit(solution)/shard_map/all_to_all | solution.py:43
  94.8 14.5 %copy.44 = bf16[1,6,256,16,256]{2,1,4,3,0:T(8,128)(2,1)} copy(bf16[1,6,256,16,256]{2,4,3,1,0:T(8,128)(2,1)} %get-tuple-element.11) | data formatting | bytes 25165824 | tf_op jit(solution)/shard_map/jit(take_along_axis)/select_n | solution.py:18
  109.3 235.3 %all-to-all-done = bf16[1,6,256,4096]{2,1,0,3:T(8,128)(2,1)} async-done(((bf16[1,6,256,4096]{2,1,0,3:T(8,128)(2,1)}), bf16[1,6,256,4096]{2,1,0,3:T(8,128)(2,1)}, u32[]{:S(2)}, u32[]{:S(2)}) %all-to-all-start) | async-done | bytes 12582944 | tf_op jit(solution)/shard_map/all_to_all | solution.py:43
  344.6 0.0 copy-start.2
  344.6 5.3 all-to-all-start.1
  349.9 0.2 all-reduce.2.cloned.1.call-start
  350.1 0.0 copy-done.2
  350.1 0.1 clamp_shift-left_fusion.1
  350.2 0.1 reshape.382
  350.3 0.1 clamp_shift-left_fusion
  350.4 0.1 reshape.387
  350.5 11.7 %gather_fusion.2 = bf16[96,256,256]{2,1,0:T(8,128)(2,1)} fusion(bf16[6,16,256,256]{3,2,1,0:T(8,128)(2,1)} %param.12, s32[96]{0:T(128)S(1)} %reshape.387), kind=kCustom, calls=%fused_computation.2.clone | custom fusion | bytes 25166592 | tf_op jit(solution)/shard_map/jit(take_along_axis)/gather | solution.py:31
  362.2 0.1 and_bitcast_fusion
  362.2 0.1 and_bitcast_fusion.1
  362.3 22.0 %copy.40 = bf16[1,6,256,16,256]{4,2,3,1,0:T(8,128)(2,1)} copy(bf16[1,6,256,16,256]{2,1,4,3,0:T(8,128)(2,1)} %bitcast.11) | data formatting | bytes 25165824 | tf_op jit(solution)/shard_map/all_to_all | solution.py:43
  384.3 210.4 %all-to-all-done.1 = bf16[1,6,256,4096]{2,1,0,3:T(8,128)(2,1)} async-done(((bf16[1,6,256,4096]{2,1,0,3:T(8,128)(2,1)}), bf16[1,6,256,4096]{2,1,0,3:T(8,128)(2,1)}, u32[]{:S(2)}, u32[]{:S(2)}) %all-to-all-start.1) | async-done | bytes 12582944 | tf_op jit(solution)/shard_map/all_to_all | solution.py:43
  594.8 22.0 %copy.46 = bf16[1,6,256,16,256]{4,2,3,1,0:T(8,128)(2,1)} copy(bf16[1,6,256,16,256]{2,1,4,3,0:T(8,128)(2,1)} %bitcast.33) | data formatting | bytes 25165824 | tf_op jit(solution)/shard_map/all_to_all | solution.py:43
  616.8 11.7 %gather_fusion.1 = bf16[96,256,256]{2,1,0:T(8,128)(2,1)} fusion(bf16[6,16,256,256]{3,2,1,0:T(8,128)(2,1)} %bitcast.78, s32[96]{0:T(128)S(1)} %reshape.382), kind=kCustom, calls=%fused_computation.1.clone | custom fusion | bytes 25166592 | tf_op jit(solution)/shard_map/jit(take_along_axis)/gather | solution.py:30
  628.5 11.8 %gather_fusion.4 = bf16[96,256,256]{2,1,0:T(8,128)(2,1)} fusion(bf16[6,16,256,256]{3,2,1,0:T(8,128)(2,1)} %bitcast.79, s32[96]{0:T(128)S(1)} %reshape.382), kind=kCustom, calls=%fused_computation.4.clone | custom fusion | bytes 25166592 | tf_op jit(solution)/shard_map/jit(take_along_axis)/gather | solution.py:30
  640.2 0.0 copy-start
  640.3 12.5 %fusion.2 = f32[16,256,256,1]{1,2,0,3:T(8,128)} fusion(bf16[1,6,16,256,256]{4,3,2,1,0:T(8,128)(2,1)} %bitcast.85, pred[6,16]{1,0:T(8,128)(4,1)S(1)} %and_bitcast_fusion.1, bf16[6,16,256,256]{3,2,1,0:T(8,128)(2,1)} %bitcast.82, pred[6,16]{1,0:T(8,128)(4,1)S(1)} %and_bitcast_fusion), kind=kOutput, calls=%fused_computation.7 | convolution fusion | flops 3233808384 | bytes 29360320 | tf_op jit(solution)/shard_map/tnab,vtnbc->vnac/dot_general | solution.py:32
  652.7 0.8 copy-done
  653.5 8.8 %fusion = f32[16,256,256,1]{1,2,0,3:T(8,128)} fusion(bf16[1,6,16,256,256]{4,3,2,1,0:T(8,128)(2,1)S(1)} %bitcast.84, pred[6,16]{1,0:T(8,128)(4,1)S(1)} %and_bitcast_fusion.1, bf16[6,16,256,256]{3,2,1,0:T(8,128)(2,1)} %bitcast.83, pred[6,16]{1,0:T(8,128)(4,1)S(1)} %and_bitcast_fusion), kind=kOutput, calls=%fused_computation.5 | convolution fusion | flops 3233808384 | bytes 29360320 | tf_op jit(solution)/shard_map/tnab,vtnbc->vnac/dot_general | solution.py:32
  662.4 7.2 pad_maximum_fusion
  669.6 0.0 all-reduce.2.cloned.1.call-update
  669.6 104.8 %all-reduce.2.cloned.1.call-done = f32[2,4096,256]{2,1,0:T(8,128)} async-done(((f32[2,4096,256]{2,1,0:T(8,128)}), f32[2,4096,256]{2,1,0:T(8,128)}) %all-reduce.2.cloned.1.call-update) | async-done | bytes 8388624 | tf_op jit(solution)/shard_map/psum | solution.py:46
  774.4 2.3 constant_dynamic-slice_fusion
  (3 shorter events, 0.1 us)
Async XLA Ops:
  18.6 10.2 %copy-start.1 = (bf16[1,256,4096]{1,2,0:T(8,128)(2,1)S(1)}, bf16[1,256,4096]{1,2,0:T(8,128)(2,1)}, u32[]{:S(2)}) copy-start(bf16[1,256,4096]{1,2,0:T(8,128)(2,1)} %copy.61) | copy-start | bytes 6291460
  86.8 257.7 %all-to-all-start = ((bf16[1,6,256,4096]{2,1,0,3:T(8,128)(2,1)}), bf16[1,6,256,4096]{2,1,0,3:T(8,128)(2,1)}, u32[]{:S(2)}, u32[]{:S(2)}) async-start(bf16[1,6,256,4096]{2,1,0,3:T(8,128)(2,1)} %bitcast.77), calls=%async_computation | async-start | bytes 33554432 | tf_op jit(solution)/shard_map/all_to_all | solution.py:43
  344.6 5.5 copy-start.2
  344.6 250.2 %all-to-all-start.1 = ((bf16[1,6,256,4096]{2,1,0,3:T(8,128)(2,1)}), bf16[1,6,256,4096]{2,1,0,3:T(8,128)(2,1)}, u32[]{:S(2)}, u32[]{:S(2)}) async-start(bf16[1,6,256,4096]{2,1,0,3:T(8,128)(2,1)} %bitcast.76), calls=%async_computation.1 | async-start | bytes 33554432 | tf_op jit(solution)/shard_map/all_to_all | solution.py:43
  349.9 424.6 %all-reduce.2.cloned.1.call-start = ((), (), s32[]{:S(2)}) async-start(), calls=%async_computation.2 | async-start | bytes 16777216 | tf_op jit(solution)/shard_map/psum | solution.py:46
  640.2 13.3 %copy-start = (bf16[96,256,256]{2,1,0:T(8,128)(2,1)S(1)}, bf16[96,256,256]{2,1,0:T(8,128)(2,1)}, u32[]{:S(2)}) copy-start(bf16[96,256,256]{2,1,0:T(8,128)(2,1)} %gather_fusion.4) | copy-start | bytes 37748740
Sparse Core Ops, SparseCore 0:
  669.7 104.6 all-reduce.1
where the time goes:
time: 786 us; the launch traced here: 784 us
  waiting for transfers between devices  550 us (70%)
  local copies, waits for them, and re-layouts  142 us (18%)
  matrix products  41.3 us (5%)
  other arithmetic  22.8 us (3%)
  starting transfers between devices  13.5 us (2%)
  between operations  13.5 us (2%)
    all_to_all x2, waiting for transfers between devices, per_device(): lax.all_to_all(outgoing, 'blocks', split_axis=3, concat_axis=2, tiled=True)  446 us
    psum x1, waiting for transfers between devices, per_device(): totals = lax.psum(partial_value, 'terms')  105 us
    all_to_all x2, local copies, waits for them, and re-layouts, per_device(): lax.all_to_all(outgoing, 'blocks', split_axis=3, concat_axis=2, tiled=True)  44.1 us
    select_n x2, local copies, waits for them, and re-layouts, first_section(): jnp.take_along_axis(product, positions[None, :, None, :, None], axis=3)  25.6 us
    gather x3, local copies, waits for them, and re-layouts, second_section(): jnp.take_along_axis(blocked, positions[None, :, :, None, None], axis=2)  23.5 us
    gather x3, local copies, waits for them, and re-layouts, first_section(): jnp.take_along_axis(product, positions[None, :, None, :, None], axis=3)  23.5 us
    dot_general x2, matrix products, second_section(): jnp.einsum('tnab,vtnbc->vnac', moved_left, moved_blocks, preferred_elemen...  21.3 us
    dot_general x2, matrix products, first_section(): jnp.einsum('vrnb,tnbc->vtrnc', blocked, right_ops, preferred_element_type...  20 us
  transfers between devices with their start and end apart: 3, of which 3 were waited for; matrix products, arithmetic and copies ran while one was open for 6% of the time, Pallas kernels for 0%

commit v1 on v0

v1 whole, which is shorter than its diff:
```python
import functools

import jax
import jax.numpy as jnp
from jax import lax
from jax.experimental import pallas as pl
from jax.experimental.pallas import tpu as pltpu
from jax.sharding import PartitionSpec as P

MESH = pl.DeviceIdType.MESH
ANY = pl.BlockSpec(memory_space=pl.ANY)
SMEM = pl.BlockSpec(memory_space=pltpu.SMEM)
VMEM = pl.BlockSpec(memory_space=pltpu.VMEM)
B = 256
MIB = 1024 * 1024


def place():
    terms = lax.axis_index("terms")
    blocks = lax.axis_index("blocks")
    return terms // 2, terms % 2, blocks // 4, blocks % 4


def at(y, core, z, x):
    return (lax.rem(y + 4, 4) * 2 + core, lax.rem(z + 4, 4) * 4 + lax.rem(x + 4, 4))


def remote(source, target, send, recv, device):
    return pltpu.make_async_remote_copy(
        src_ref=source,
        dst_ref=target,
        send_sem=send,
        recv_sem=recv,
        device_id=device,
        device_id_type=MESH,
    )


def greet(devices):
    barrier = pltpu.get_barrier_semaphore()
    for device in devices:
        pl.semaphore_signal(barrier, inc=1, device_id=device, device_id_type=MESH)
    pl.semaphore_wait(barrier, len(devices))


SHARED = 4
DIRECT = 6


def gather_kernel(
    shifts, shift_row, psi, left, right,
    rows, lefts, rights, other_row,
    right_in, picked,
    x_send, x_recv, y_send, y_recv, c_send, c_recv, l_sem, r_sem,
):
    y, core, z, x = place()
    x_up, x_down = at(y, core, z, x + 1), at(y, core, z, x - 1)
    y_up, y_down = at(y + 1, core, z, x), at(y - 1, core, z, x)
    partner = at(y, 1 - core, z, x)
    greet([x_up, x_down, y_up, y_down, partner])

    def item(index, owner):
        if index < 2:
            return 2 * owner + index, 0, 256
        if index < SHARED:
            return 6 + index, pl.multiple_of(owner * 64, 64), 64
        return 6 + index, 0, 256

    def held(index, owner, member, part=None):
        sector, start, count = item(index, owner)
        if part is not None:
            count = count // 2
            start = start + part * count
        return rows.at[sector, lax.rem(member + 4, 4), pl.ds(start, count)]

    def own(index):
        sector, start, count = item(index, y)
        column = pl.multiple_of(sector * B, B) if index < 2 else sector * B
        return psi.at[core, pl.ds(start, count), pl.ds(column, B)]

    waiting = []

    def x_copy(index, kind, source, target, device):
        copy = remote(source, target, x_send.at[index, kind], x_recv.at[index, kind], device)
        copy.start()
        waiting.append(copy)
        return copy

    def y_copy(index, which, kind, source, device):
        copy = remote(
            source, source, y_send.at[index, which, kind], y_recv.at[index, which, kind], device
        )
        copy.start()
        waiting.append(copy)
        return copy

    def x_first(index):
        target = held(index, y, x)
        return (
            x_copy(index, 0, own(index), target, x_up),
            x_copy(index, 1, own(index), target, x_down),
        )

    def x_forward_up(index):
        block = held(index, y, x - 1, 0)
        return x_copy(index, 2, block, block, x_up)

    def x_forward_down(index):
        block = held(index, y, x + 1, 1)
        return x_copy(index, 3, block, block, x_down)

    def y_first(index, which, member):
        block = held(index, y, member)
        return (
            y_copy(index, which, 0, block, y_up),
            y_copy(index, which, 1, block, y_down),
        )

    def y_forward_up(index, which, member):
        return y_copy(index, which, 2, held(index, lax.rem(y + 3, 4), member, 0), y_up)

    def y_forward_down(index, which, member):
        return y_copy(index, which, 3, held(index, lax.rem(y + 1, 4), member, 1), y_down)

    first = [x_first(index) for index in range(SHARED)]
    local = []
    load = pltpu.make_async_copy(right, right_in, r_sem)
    load.start()
    swap = remote(shift_row, other_row, c_send.at[0], c_recv.at[0], partner)
    swap.start()
    waiting.append(swap)
    mine = left.at[:, pl.ds(4 * z, 4)]
    swap_left = remote(mine, lefts.at[pl.ds(6, 6)], c_send.at[1], c_recv.at[1], partner)
    swap_left.start()
    waiting.append(swap_left)
    copy = pltpu.make_async_copy(mine, lefts.at[pl.ds(0, 6)], l_sem.at[0])
    copy.start()
    local.append(copy)
    for sector in range(16):
        copy = pltpu.make_async_copy(
            psi.at[core, :, pl.ds(sector * B, B)], rows.at[sector, x], l_sem.at[1 + sector]
        )
        copy.start()
        local.append(copy)

    members = [x - 1, x + 1, x + 2]
    forward = []
    y_list = {}
    for index in range(SHARED):
        up, down = first[index]
        up.wait_recv()
        one = x_forward_up(index)
        y_list[index, 0] = y_first(index, 0, members[0])
        down.wait_recv()
        two = x_forward_down(index)
        y_list[index, 1] = y_first(index, 1, members[1])
        forward.append((one, two))
    direct = [x_first(index) for index in range(SHARED, SHARED + DIRECT)]

    load.wait()
    for term in range(6):
        shift = shifts[term]
        for k in range(4):
            picked[term, k] = right_in[term, (x + 4 * k + shift) & 15]
    swap_right = remote(picked, rights.at[pl.ds(6, 6)], c_send.at[2], c_recv.at[2], partner)
    swap_right.start()
    waiting.append(swap_right)
    copy = pltpu.make_async_copy(picked, rights.at[pl.ds(0, 6)], l_sem.at[17])
    copy.start()
    local.append(copy)

    for index in range(SHARED):
        for copy in forward[index]:
            copy.wait_recv()
        y_list[index, 2] = y_first(index, 2, members[2])

    last = []

    def y_second(index, which):
        up, down = y_list[index, which]
        up.wait_recv()
        last.append(y_forward_up(index, which, members[which]))
        down.wait_recv()
        last.append(y_forward_down(index, which, members[which]))

    def x_second(index):
        up, down = direct[index - SHARED]
        up.wait_recv()
        last.append(x_forward_up(index))
        down.wait_recv()
        last.append(x_forward_down(index))

    order = [(index, which) for which in range(3) for index in range(SHARED)]
    while order or direct:
        for _ in range(2):
            if order:
                y_second(*order.pop(0))
        index = SHARED + DIRECT - len(direct) if direct else None
        if direct:
            up, down = direct.pop(0)
            up.wait_recv()
            last.append(x_forward_up(index))
            down.wait_recv()
            last.append(x_forward_down(index))
    for copy in last:
        copy.wait_recv()
    swap.wait_recv()
    swap_left.wait_recv()
    swap_right.wait_recv()
    for copy in waiting:
        copy.wait_send()
    for copy in local:
        copy.wait()


def gather(shifts, psi, left, right):
    row = jnp.zeros((8, 128), jnp.int32).at[0, :6].set(shifts)
    half = jnp.bfloat16
    return pl.pallas_call(
        gather_kernel,
        out_shape=(
            jax.ShapeDtypeStruct((16, 4, B, B), half),
            jax.ShapeDtypeStruct((12, 4, B, B), half),
            jax.ShapeDtypeStruct((12, 4, B, B), half),
            jax.ShapeDtypeStruct((8, 128), jnp.int32),
        ),
        in_specs=[SMEM, ANY, ANY, ANY, ANY],
        out_specs=(ANY, ANY, ANY, ANY),
        scratch_shapes=[
            pltpu.VMEM((6, 16, B, B), half),
            pltpu.VMEM((6, 4, B, B), half),
            pltpu.SemaphoreType.DMA((SHARED + DIRECT, 4)),
            pltpu.SemaphoreType.DMA((SHARED + DIRECT, 4)),
            pltpu.SemaphoreType.DMA((SHARED, 3, 4)),
            pltpu.SemaphoreType.DMA((SHARED, 3, 4)),
            pltpu.SemaphoreType.DMA((3,)),
            pltpu.SemaphoreType.DMA((3,)),
            pltpu.SemaphoreType.DMA((18,)),
            pltpu.SemaphoreType.DMA,
        ],
        compiler_params=pltpu.CompilerParams(
            collective_id=0, has_side_effects=True, vmem_limit_bytes=40 * MIB
        ),
        name="gather",
    )(shifts, row, psi, left, right)


def product_kernel(shifts, other_row, place_ref, rows, lefts, rights, out, total, moved):
    term = pl.program_id(0)
    z, x = place_ref[0], place_ref[1]

    @pl.when(term == 0)
    def _():
        total[...] = jnp.zeros_like(total)

    shift = jnp.where(term < 6, shifts[jnp.minimum(term, 5)], other_row[0, jnp.maximum(term - 6, 0)])
    for k in range(4):
        sector = (x + 4 * k + shift) & 15
        moved[k] = jnp.dot(
            rows[sector].reshape(4 * B, B), rights[0, k], preferred_element_type=jnp.float32
        ).astype(jnp.bfloat16)
    for i in range(4):
        row = (4 * z + i + shift) & 15
        for k in range(4):
            total[k, row] += jnp.dot(
                lefts[0, i], moved[k, i * B : (i + 1) * B], preferred_element_type=jnp.float32
            )

    @pl.when(term == 11)
    def _():
        out[...] = total[...].astype(jnp.bfloat16)


def products(shifts, other_row, rows, lefts, rights):
    blocks = lax.axis_index("blocks")
    where = jnp.stack([blocks // 4, blocks % 4]).astype(jnp.int32)
    return pl.pallas_call(
        product_kernel,
        grid=(12,),
        out_shape=jax.ShapeDtypeStruct((4, 16, B, B), jnp.bfloat16),
        in_specs=[
            SMEM,
            SMEM,
            SMEM,
            VMEM,
            pl.BlockSpec((1, 4, B, B), lambda t: (t, 0, 0, 0)),
            pl.BlockSpec((1, 4, B, B), lambda t: (t, 0, 0, 0)),
        ],
        out_specs=VMEM,
        scratch_shapes=[
            pltpu.VMEM((4, 16, B, B), jnp.float32),
            pltpu.VMEM((4, 4 * B, B), jnp.bfloat16),
        ],
        compiler_params=pltpu.CompilerParams(vmem_limit_bytes=56 * MIB),
        name="products",
    )(shifts, other_row, where, rows, lefts, rights)


OFFSETS = (2, 1, -1, 0)


def reduce_kernel(
    part, out, held, relayed, onward, first, second_out, second, sums,
    load, rel_send, rel_recv, fwd_send, fwd_recv, dir_send, dir_recv, two_send, two_recv,
    c_send, c_recv,
):
    y, core, z, x = place()
    partner = at(y, 1 - core, z, x)
    here = ((y, z), (z, y))

    def on_first(half, step):
        return at(y + step, core, z, x) if half == 0 else at(y, core, z + step, x)

    def on_second(half, step):
        return at(y, core, z + step, x) if half == 0 else at(y + step, core, z, x)

    greet([at(y + d, core, z, x) for d in (1, 2, 3)] + [at(y, core, z + d, x) for d in (1, 2, 3)] + [partner])

    def block(ref, half, step, turn, part_of=None):
        a = lax.rem(here[half][0] + step + 4, 4)
        o = lax.rem(here[half][1] + OFFSETS[turn] + 4, 4)
        y_of, z_of = (a, o) if half == 0 else (o, a)
        if part_of is None:
            return ref.at[z_of, y_of, half]
        return ref.at[z_of, y_of, half, pl.ds(part_of * 256, 256)]

    sent = []

    def start(copy):
        copy.start()
        sent.append(copy)
        return copy

    relays, straight = {}, {}
    for turn in range(4):
        for half in range(2):
            up, down = on_first(half, 1), on_first(half, -1)
            relays[half, turn] = tuple(
                start(remote(
                    block(part, half, 2, turn, way), relayed.at[half, way, turn],
                    rel_send.at[half, way, turn], rel_recv.at[half, way, turn], device,
                ))
                for way, device in enumerate((up, down))
            )
            straight[half, turn] = tuple(
                start(remote(
                    block(part, half, step, turn, 1 - way),
                    first.at[half, way, turn, pl.ds((1 - way) * 256, 256)],
                    dir_send.at[half, way, turn], dir_recv.at[half, way, turn], device,
                ))
                for way, step, device in ((0, 1, up), (1, -1, down))
            )
    fill = pltpu.make_async_copy(part, held, load)
    fill.start()
    fill.wait()

    forwards = {}
    for turn in range(4):
        for half in range(2):
            copies = []
            for way, step in ((0, 1), (1, -1)):
                relays[half, turn][way].wait_recv()
                mine = block(held, half, step, turn, way)[...]
                total = mine.astype(jnp.float32) + relayed[half, way, turn].astype(jnp.float32)
                onward[half, way, turn] = total.astype(jnp.bfloat16)
                copies.append(start(remote(
                    onward.at[half, way, turn], first.at[half, way, turn, pl.ds(way * 256, 256)],
                    fwd_send.at[half, way, turn], fwd_recv.at[half, way, turn], on_first(half, step),
                )))
            forwards[half, turn] = copies

    seconds = {}
    for turn in range(4):
        for half in range(2):
            for way in range(2):
                straight[half, turn][way].wait_recv()
                forwards[half, turn][way].wait_recv()
            total = (
                block(held, half, 0, turn)[...].astype(jnp.float32)
                + first[half, 0, turn].astype(jnp.float32)
                + first[half, 1, turn].astype(jnp.float32)
            )
            if turn < 3:
                second_out[half, turn] = total.astype(jnp.bfloat16)
                seconds[half, turn] = start(remote(
                    second_out.at[half, turn], second.at[half, turn],
                    two_send.at[half, turn], two_recv.at[half, turn],
                    on_second(half, OFFSETS[turn]),
                ))
            else:
                sums[half] = total
    for half in range(2):
        for turn in range(3):
            seconds[half, turn].wait_recv()
        sums[half] = (
            sums[half]
            + second[half, 0].astype(jnp.float32)
            + second[half, 1].astype(jnp.float32)
            + second[half, 2].astype(jnp.float32)
        )
    swap = start(remote(sums.at[1 - core], out.at[core], c_send, c_recv, partner))
    out[core] = sums[core]
    swap.wait_recv()
    for copy in sent:
        copy.wait_send()


def reduce(part):
    half = jnp.bfloat16
    dma = pltpu.SemaphoreType.DMA
    return pl.pallas_call(
        reduce_kernel,
        out_shape=jax.ShapeDtypeStruct((2, 512, B), jnp.float32),
        in_specs=[ANY],
        out_specs=VMEM,
        scratch_shapes=[
            pltpu.VMEM((4, 4, 2, 512, B), half),
            pltpu.VMEM((2, 2, 4, B, B), half),
            pltpu.VMEM((2, 2, 4, B, B), half),
            pltpu.VMEM((2, 2, 4, 512, B), half),
            pltpu.VMEM((2, 3, 512, B), half),
            pltpu.VMEM((2, 3, 512, B), half),
            pltpu.VMEM((2, 512, B), jnp.float32),
            dma,
            dma((2, 2, 4)),
            dma((2, 2, 4)),
            dma((2, 2, 4)),
            dma((2, 2, 4)),
            dma((2, 2, 4)),
            dma((2, 2, 4)),
            dma((2, 3)),
            dma((2, 3)),
            dma,
            dma,
        ],
        compiler_params=pltpu.CompilerParams(
            collective_id=1, has_side_effects=True, vmem_limit_bytes=48 * MIB
        ),
        name="reduce",
    )(part.reshape(4, 4, 2, 512, B))


def per_device(psi, shifts, left_ops, right_ops):
    rows, lefts, rights, other_row = gather(shifts, psi, left_ops, right_ops)
    part = products(shifts, other_row, rows, lefts, rights)
    return reduce(part)


def solution(mesh):
    in_specs = (
        P(None, "blocks", None),
        P("terms"),
        P("terms", None, None, None),
        P("terms", None, None, None),
    )
    out_specs = P(None, "terms", "blocks")
    return jax.shard_map(
        per_device, mesh=mesh, in_specs=in_specs, out_specs=out_specs, check_vma=False
    )
```

time: 786 us -> 132 us (0.17)
  waiting for transfers between devices: 550 us -> 0 us
  local copies, waits for them, and re-layouts: 142 us -> 7.71 us
  Pallas kernels: 0 us -> 123 us
  matrix products: 41.3 us -> 0 us
  other arithmetic: 22.8 us -> 0.64 us
  starting transfers between devices: 13.5 us -> 0 us
  between operations: 13.5 us -> 0.03 us
    all_to_all x2 -> x0, waiting for transfers between devices: 446 us -> none  [per_device(): lax.all_to_all(outgoing, 'blocks', split_axis=3, concat_axis=2, tiled=True)]
    pallas_call x0 -> x3, Pallas kernels: none -> 123 us  [the longest x1 53.3 us: reduce(): pl.pallas_call(reduce_kernel, out_shape=jax.ShapeDtypeStruct((2, 512, B),...]
    psum x1 -> x0, waiting for transfers between devices: 105 us -> none  [per_device(): totals = lax.psum(partial_value, 'terms')]
    gather x8 -> x0, local copies, waits for them, and re-layouts: 58.8 us -> none  [the longest x3 23.5 us: second_section(): jnp.take_along_axis(blocked, positions[None, :, :, None, None], axis=2)]
    all_to_all x2 -> x0, local copies, waits for them, and re-layouts: 44.1 us -> none  [per_device(): lax.all_to_all(outgoing, 'blocks', split_axis=3, concat_axis=2, tiled=True)]
    dot_general x4 -> x0, matrix products: 41.3 us -> none  [the longest x2 21.3 us: second_section(): jnp.einsum('tnab,vtnbc->vnac', moved_left, moved_blocks, preferred_elemen...]
    select_n x2 -> x0, local copies, waits for them, and re-layouts: 25.6 us -> none  [first_section(): jnp.take_along_axis(product, positions[None, :, None, :, None], axis=3)]
    select_n x1 -> x0, other arithmetic: 13.7 us -> none  [first_section(): jnp.take_along_axis(product, positions[None, :, None, :, None], axis=3)]
  transfers between devices with their start and end apart: 3 -> 0, of which waited for: 3 -> 0; matrix products, arithmetic and copies ran while one was open for 6% -> 0% of each run, Pallas kernels for 0% -> 0%
where the time goes in v1:
time: 132 us; the launch traced here: 131 us
  Pallas kernels  123 us (93%)
  local copies, waits for them, and re-layouts  7.71 us (6%)
    pallas_call x1, Pallas kernels, reduce(): pl.pallas_call(reduce_kernel, out_shape=jax.ShapeDtypeStruct((2, 512, B),...  53.3 us
    pallas_call x1, Pallas kernels, gather(): pl.pallas_call(gather_kernel, out_shape=(jax.ShapeDtypeStruct((16, 4, B,...  44.7 us
    pallas_call x1, Pallas kernels, products(): pl.pallas_call(product_kernel, grid=(12,), out_shape=jax.ShapeDtypeStruct...  24.5 us
    unnamed x9, local copies, waits for them, and re-layouts  7.05 us

profile of v1, /device:TPU:0, one launch (start us, length us, event | category | flops | bytes accessed | tf_op | source)
XLA Modules:
  0.0 130.9 jit_solution(6719157711107979491)
XLA Ops:
  0.0 0.6 pad_add_fusion.place_ref
  0.6 0.7 scatter.4.shift_row
  1.3 0.0 copy-start.1
  1.3 2.2 %copy-done.1 = bf16[2,256,4096]{2,1,0:T(8,128)(2,1)S(1)} copy-done((bf16[2,256,4096]{2,1,0:T(8,128)(2,1)S(1)}, bf16[2,256,4096]{2,1,0:T(8,128)(2,1)}, u32[]{:S(2)}) %copy-start.1) | copy-done | bytes 4194328
  3.5 0.0 copy-start.2
  3.5 0.7 copy-done.2
  4.1 44.7 %gather.1 = (bf16[16,4,256,256]{3,2,1,0:T(8,128)(2,1)}, bf16[12,4,256,256]{3,2,1,0:T(8,128)(2,1)S(1)}, bf16[12,4,256,256]{3,2,1,0:T(8,128)(2,1)}, s32[8,128]{1,0:T(8,128)S(1)}) custom-call(s32[6]{0:T(128)S(1)} %copy-done.2, s32[8,128]{1,0:T(8,128)S(1)} %scatter.4.shift_row, bf16[2,256,4096]{2,1,0:T(8,128)(2,1)S(1)} %copy-done.1, ...), custom_call_target="tpu_custom_call" | custom-call | tf_op jit(solution)/shard_map/gather/pallas_call | solution.py:219
  48.9 0.0 copy-start
  48.9 2.6 %copy-done = bf16[12,4,256,256]{3,2,1,0:T(8,128)(2,1)} copy-done((bf16[12,4,256,256]{3,2,1,0:T(8,128)(2,1)}, bf16[12,4,256,256]{3,2,1,0:T(8,128)(2,1)S(1)}, u32[]{:S(2)}) %copy-start) | copy-done | bytes 6291480
  51.5 0.0 copy-start.3
  51.5 0.6 copy-done.3
  52.1 24.5 %products.1 = bf16[4,16,256,256]{3,2,1,0:T(8,128)(2,1)} custom-call(s32[6]{0:T(128)} %shifts.3, s32[8,128]{1,0:T(8,128)} %copy-done.3, s32[2]{0:T(128)} %pad_add_fusion.place_ref, bf16[16,4,256,256]{3,2,1,0:T(8,128)(2,1)} %get-tuple-element.22.rows, bf16[12,4,256,256]{3,2,1,0:T(8,128)(2,1)} %copy-done, bf16[12,4,256,256]{3,2,1,0:T(8,128)(2,1)} %get-tuple-element.24.rights), custom_call_target="tpu_custom_call" | custom-call | tf_op jit(solution)/shard_map/products/pallas_call | solution.py:277
  76.6 53.3 %reduce.3 = f32[2,512,256]{2,1,0:T(8,128)S(1)} custom-call(bf16[4,4,2,512,256]{4,3,2,1,0:T(8,128)(2,1)} %bitcast.5), custom_call_target="tpu_custom_call" | custom-call | tf_op jit(solution)/shard_map/reduce/pallas_call | solution.py:411
  129.9 1.0 copy.6
Async XLA Ops:
  1.3 2.2 %copy-start.1 = (bf16[2,256,4096]{2,1,0:T(8,128)(2,1)S(1)}, bf16[2,256,4096]{2,1,0:T(8,128)(2,1)}, u32[]{:S(2)}) copy-start(bf16[2,256,4096]{2,1,0:T(8,128)(2,1)} %psi.1) | copy-start | bytes 12582916
  3.5 0.7 copy-start.2
  48.9 2.6 %copy-start = (bf16[12,4,256,256]{3,2,1,0:T(8,128)(2,1)}, bf16[12,4,256,256]{3,2,1,0:T(8,128)(2,1)S(1)}, u32[]{:S(2)}) copy-start(bf16[12,4,256,256]{3,2,1,0:T(8,128)(2,1)S(1)} %get-tuple-element.23.lefts) | copy-start | bytes 18874372
  51.5 0.6 copy-start.3

commit v2 on v0

v2 whole, which is shorter than its diff:
```python
import jax
import jax.numpy as jnp
from jax import lax
from jax.experimental import pallas as pl
from jax.experimental.pallas import tpu as pltpu
from jax.sharding import PartitionSpec as P

MESH = pl.DeviceIdType.MESH
B = 256
QUARTER = 64
MIB = 1024 * 1024
F32 = jnp.float32
BF16 = jnp.bfloat16

OFFSETS = (2, 1, -1, 0)
WIDTH = (2, 1)
PIECES = (2, 3)


def wrap(value):
    return lax.rem(value + 4, 4)


def kernel(
    shifts, shift_row, psi, left, right, out,
    q_first, q_last, packed, picked, moved, held, stage_even, stage_odd, shift_all, shift_words,
    far, near, relayed, onward, first, second_out, second,
    x_send, x_recv, z_send, z_recv, y_send, y_recv, d_send, d_recv, o_send, o_recv,
    local_sem, stage_sem, shift_sem,
    rel_send, rel_recv, dir_send, dir_recv, fwd_send, fwd_recv, two_send, two_recv,
):
    q, staged = (q_first, q_last), (stage_even, stage_odd)
    terms = lax.axis_index("terms")
    blocks = lax.axis_index("blocks")
    y, core, z, x = terms // 2, terms % 2, blocks // 4, blocks % 4

    def on(dy=0, dz=0, dx=0):
        return (wrap(y + dy) * 2 + core, wrap(z + dz) * 4 + wrap(x + dx))

    partner = (y * 2 + 1 - core, blocks)
    everyone = [on(dy=d) for d in (1, 2, 3)] + [on(dx=d) for d in (1, 2, 3)]
    everyone += [on(dz=1), on(dz=-1), partner]

    tile = pl.ds(pl.multiple_of(128 * (x // 2), 128), 128)

    def fill_right(term):
        copy = pltpu.make_async_copy(right.at[term], staged[term % 2], stage_sem.at[term])
        copy.start()
        return copy

    def fill_left(pair):
        copies = []
        for k in range(2):
            copy = pltpu.make_async_copy(
                left.at[2 * pair + k, :, :, tile],
                staged[pair % 2].at[:, :, pl.ds(128 * k, 128)],
                stage_sem.at[6 + 2 * pair + k],
            )
            copy.start()
            copies.append(copy)
        return copies

    loads = {0: fill_right(0), 1: fill_right(1)}
    row_copy = pltpu.make_async_copy(shift_row, shift_all.at[0], shift_sem.at[0])
    row_copy.start()
    barrier = pltpu.get_barrier_semaphore()
    for device in everyone:
        pl.semaphore_signal(barrier, inc=1, device_id=device, device_id_type=MESH)
    pl.semaphore_wait(barrier, len(everyone))

    def send(source, target, semaphores, index, device):
        copy = pltpu.make_async_remote_copy(
            src_ref=source,
            dst_ref=target,
            send_sem=semaphores[0],
            recv_sem=semaphores[1].at[index],
            device_id=device,
            device_id_type=MESH,
        )
        copy.start()
        return copy

    xs = [(x_send.at[v], x_recv) for v in range(2)]
    zs = [(z_send.at[v], z_recv) for v in range(2)]
    ys = [(y_send.at[v], y_recv) for v in range(2)]
    ds = [(d_send.at[v], d_recv) for v in range(2)]
    os = [(o_send.at[k], o_recv) for k in range(3)]
    base = 2048 * core
    me = 4 * z + x

    groups = (z, wrap(z - 1), wrap(z + 1), wrap(z + 2))
    state = {}

    def lanes(v, owner):
        return pl.ds(pl.multiple_of(base + 128 * WIDTH[v] * owner, 128), 128 * WIDTH[v])

    def all_lanes(v):
        return pl.ds(pl.multiple_of(base, 128), 512 * WIDTH[v])

    def piece_lanes(v, number):
        width = (2048 - 512 * WIDTH[v]) // PIECES[v]
        return pl.ds(pl.multiple_of(base + 512 * WIDTH[v] + width * number, 128), width)

    def rows_of(v, zz, window, half=None):
        if half is None:
            return q[v].at[pl.ds(4 * zz, 4), :, window]
        return q[v].at[pl.ds(4 * zz + 2 * half, 2), :, window]

    def x_part(v, number, window):
        def source(member):
            return psi.at[v, pl.ds(pl.multiple_of(QUARTER * member, QUARTER), QUARTER), window]

        target = q[v].at[me, :, window]
        copies = [
            send(source(wrap(x + d)), target, xs[v], (v, number, d - 1), on(dx=d)) for d in (1, 3, 2)
        ]
        own = pltpu.make_async_copy(source(x), target, local_sem.at[v, number])
        own.start()
        state["x", v, number] = copies, own

    def x_done(v, number):
        copies, own = state["x", v, number]
        for copy in copies:
            copy.wait_recv()
        own.wait()

    def window_of(v, number):
        return lanes(v, y) if number == 0 else piece_lanes(v, number - 1)

    def x_start(v):
        for number in range(PIECES[v] + 1):
            x_part(v, number, window_of(v, number))

    def z_start(v, number):
        x_done(v, number)
        view = rows_of(v, z, window_of(v, number))
        state["z", v, number] = (
            send(view, view, zs[v], (v, number, 0), on(dz=1)),
            send(view, view, zs[v], (v, number, 1), on(dz=-1)),
        )
        if number == 0:
            y_start(v, 0)

    def y_start(v, g):
        view = rows_of(v, groups[g], lanes(v, y))
        state["y", v, g] = (
            send(view, view, ys[v], (v, g, 0), on(dy=1)),
            send(view, view, ys[v], (v, g, 1), on(dy=-1)),
        )

    def z_pass(v, number):
        window = window_of(v, number)
        up, down = state["z", v, number]
        up.wait_recv()
        view = rows_of(v, groups[1], window, 0)
        one = send(view, view, zs[v], (v, number, 2), on(dz=1))
        if number == 0:
            y_start(v, 1)
        down.wait_recv()
        view = rows_of(v, groups[2], window, 1)
        two = send(view, view, zs[v], (v, number, 3), on(dz=-1))
        if number == 0:
            y_start(v, 2)
        state["zz", v, number] = one, two

    def z_done(v, number):
        for copy in state["zz", v, number]:
            copy.wait_recv()
        if number == 0:
            y_start(v, 3)
        else:
            view = q[v].at[:, :, window_of(v, number)]
            state["d", v, number] = send(view, view, ds[v], (v, number - 1), partner)

    def y_pass(v, g):
        up, down = state["y", v, g]
        up.wait_recv()
        view = rows_of(v, groups[g], lanes(v, wrap(y - 1)), 0)
        one = send(view, view, ys[v], (v, g, 2), on(dy=1))
        down.wait_recv()
        view = rows_of(v, groups[g], lanes(v, wrap(y + 1)), 1)
        state["yy", v, g] = one, send(view, view, ys[v], (v, g, 3), on(dy=-1))

    def y_done(v, g):
        for copy in state["yy", v, g]:
            copy.wait_recv()
        view = rows_of(v, groups[g], all_lanes(v))
        state["d", v, -g] = send(view, view, ds[v], (v, 3 + g), partner)

    def gathered(v):
        for number in range(-3, PIECES[v] + 1):
            state["d", v, number].wait_recv()

    side = x % 2
    lower = lax.broadcasted_iota(jnp.int32, (B, 128), 1) < QUARTER

    def operators():
        swap_row = send(shift_row, shift_all.at[1], os[0], 0, partner)
        for term in range(6):
            loads[term].wait()
            for k in range(4):
                picked[term, k] = staged[term % 2][(4 * z + k + shifts[term]) & 15]
            if term < 4:
                loads[term + 2] = fill_right(term + 2)
            else:
                loads[6 + term - 4] = fill_left(term - 4)
            if term % 2 == 1:
                yield
        swap_right = send(picked.at[pl.ds(0, 6)], picked.at[pl.ds(6, 6)], os[1], 1, partner)
        for pair in range(3):
            slot = pair % 2
            for copy in loads[6 + pair]:
                copy.wait()

            def pack(i, carry, slot=slot, pair=pair):
                odd, even = staged[slot][i, :, 128:], staged[slot][i, :, :128]
                turned = jnp.where(side == 0, odd, even)
                rolled = pltpu.roll(turned.astype(F32), QUARTER, 1).astype(BF16)
                packed[pair, i] = jnp.where(lower == (side == 0), jnp.where(side == 0, even, odd), rolled)
                return carry

            for part in range(2):
                lax.fori_loop(8 * part, 8 * part + 8, pack, 0, unroll=2)
                if part == 1 and pair == 0:
                    loads[8] = fill_left(2)
                yield
        swap_left = send(packed.at[pl.ds(0, 3)], packed.at[pl.ds(3, 3)], os[2], 2, partner)
        row_copy.wait()
        swap_row.wait_recv()
        words = pltpu.make_async_copy(shift_all, shift_words, shift_sem.at[1])
        words.start()
        words.wait()
        yield
        swap_right.wait_recv()
        swap_left.wait_recv()

    def column(v, turn):
        member = wrap(x + OFFSETS[turn])
        sector = 4 * z + member

        def right_products(pair, carry):
            for k in range(2):
                term = 2 * pair + k
                shift = shift_words[term // 6, 0, term % 6]
                window = pl.ds(((sector + shift) & 15) * B, B)
                rows = [
                    q[v][(4 * wrap(y + OFFSETS[u]) + 2 * core + h - shift) & 15, :, window]
                    for u in range(4)
                    for h in range(2)
                ]
                product = jnp.dot(
                    jnp.concatenate(rows, axis=0), picked[term, member], preferred_element_type=F32
                ).astype(BF16)
                place = pl.ds(pl.multiple_of(QUARTER * term, QUARTER), QUARTER)
                for e in range(8):
                    moved[e, place, :] = product[QUARTER * e : QUARTER * (e + 1)]
            return carry

        lax.fori_loop(0, 6, right_products, 0, unroll=6)

        def left_products(e, carry):
            u, h = e // 2, e % 2
            offset = jnp.where(u == 0, 2, jnp.where(u == 1, 1, jnp.where(u == 2, 3, 0)))
            row = 4 * wrap(y + offset) + 2 * core + h
            parts = []
            for pair in range(6):
                one = shift_words[pair // 3, 0, 2 * (pair % 3)]
                two = shift_words[pair // 3, 0, 2 * (pair % 3) + 1]
                parts.append(
                    jnp.where(lower, packed[pair, (row - one) & 15], packed[pair, (row - two) & 15])
                )
            held[turn, e] = jnp.dot(
                jnp.concatenate(parts, axis=1), moved[e], preferred_element_type=F32
            )
            return carry

        lax.fori_loop(0, 8, left_products, 0, unroll=8)

    def along(half, step):
        return on(dy=step) if half == 0 else on(dx=step)

    def across(half, step):
        return on(dx=step) if half == 0 else on(dy=step)

    def value(half, ring, turn, part=None):
        column_turn, row_turn = (turn, ring) if half == 0 else (ring, turn)
        if part is None:
            return held[column_turn, 2 * row_turn + half]
        return held[column_turn, 2 * row_turn + half, 128 * part : 128 * (part + 1)]

    rels, dirs = (rel_send, rel_recv), (dir_send, dir_recv)
    fwds, twos = (fwd_send, fwd_recv), (two_send, two_recv)
    relay, straight, passed, seconds = {}, {}, {}, {}

    def emit(v, half, ring, turn):
        if ring == 0:
            far[v, half, turn] = value(half, 0, turn).astype(BF16)
            for way, step in ((0, 1), (1, -1)):
                relay[v, half, turn, way] = send(
                    far.at[v, half, turn, pl.ds(128 * way, 128)], relayed.at[v, half, way, turn],
                    rels, (v, half, way, turn), along(half, step),
                )
        elif ring < 3:
            way, step = ((0, 1), (1, -1))[ring - 1]
            near[v, half, way, turn] = value(half, ring, turn, 1 - way).astype(BF16)
            straight[v, half, turn, way] = send(
                near.at[v, half, way, turn], first.at[v, half, way, turn, pl.ds(128 * (1 - way), 128)],
                dirs, (v, half, way, turn), along(half, step),
            )

    def add(v, half, turn, way):
        relay[v, half, turn, way].wait_recv()
        total = value(half, 1 + way, turn, way) + relayed[v, half, way, turn].astype(F32)
        onward[v, half, way, turn] = total.astype(BF16)
        passed[v, half, turn, way] = send(
            onward.at[v, half, way, turn], first.at[v, half, way, turn, pl.ds(128 * way, 128)],
            fwds, (v, half, way, turn), along(half, (1, -1)[way]),
        )

    def combine(v, half, turn):
        for way in range(2):
            straight[v, half, turn, way].wait_recv()
            passed[v, half, turn, way].wait_recv()
        total = (
            value(half, 3, turn)
            + first[v, half, 0, turn].astype(F32)
            + first[v, half, 1, turn].astype(F32)
        )
        if turn < 3:
            second_out[v, half, turn] = total.astype(BF16)
            seconds[v, half, turn] = send(
                second_out.at[v, half, turn], second.at[v, half, turn],
                twos, (v, half, turn), across(half, OFFSETS[turn]),
            )
        else:
            out[v, half * B : (half + 1) * B] = total

    def finish(v, half):
        for turn in range(3):
            seconds[v, half, turn].wait_recv()
        rows = slice(half * B, (half + 1) * B)
        out[v, rows] = (
            out[v, rows]
            + second[v, half, 0].astype(F32)
            + second[v, half, 1].astype(F32)
            + second[v, half, 2].astype(F32)
        )

    def spread(v, turn):
        for ring in range(4):
            emit(v, 0, ring, turn)
            emit(v, 1, turn, ring)

    def reduce(v):
        column(v, 0)
        spread(v, 0)
        yield
        column(v, 1)
        spread(v, 1)
        yield
        for way in range(2):
            add(v, 0, 0, way)
        for turn in range(4):
            add(v, 1, turn, 0)
        yield
        column(v, 2)
        spread(v, 2)
        yield
        for way in range(2):
            add(v, 0, 1, way)
        for turn in range(4):
            add(v, 1, turn, 1)
        yield
        column(v, 3)
        spread(v, 3)
        yield
        for turn in (2, 3):
            for way in range(2):
                add(v, 0, turn, way)
            yield
        for turn in range(4):
            for half in range(2):
                combine(v, half, turn)
                yield
        finish(v, 0)
        finish(v, 1)

    ops = operators()

    def go(step, count=1):
        for _ in range(count):
            next(step, None)

    x_start(0)
    go(ops)
    z_start(0, 0)
    z_start(0, 1)
    go(ops)
    z_pass(0, 0)
    z_start(0, 2)
    x_start(1)
    go(ops, 2)
    z_done(0, 0)
    y_pass(0, 0)
    y_pass(0, 1)
    y_pass(0, 2)
    go(ops, 2)
    z_pass(0, 1)
    y_pass(0, 3)
    z_pass(0, 2)
    go(ops, 2)
    for number in range(4):
        z_start(1, number)
    for g in range(4):
        y_done(0, g)
    z_done(0, 1)
    z_done(0, 2)
    go(ops, 9)
    gathered(0)
    first_sum = reduce(0)
    go(first_sum)
    z_pass(1, 0)
    go(first_sum)
    z_done(1, 0)
    go(first_sum)
    for number in range(1, 4):
        z_pass(1, number)
    go(first_sum)
    for g in range(4):
        y_pass(1, g)
    go(first_sum)
    for number in range(1, 4):
        z_done(1, number)
    go(first_sum)
    for g in range(4):
        y_done(1, g)
    go(first_sum, 100)
    gathered(1)
    go(reduce(1), 100)

    def left_all(semaphore, ref):
        pltpu.make_async_copy(ref, ref, semaphore).wait()

    for v in range(2):
        fetched = 2048 - 384 * WIDTH[v]
        left_all(x_send.at[v], q[v].at[pl.ds(0, 3), :, pl.ds(0, fetched)])
        left_all(z_send.at[v], q[v].at[pl.ds(0, 12), :, pl.ds(0, fetched)])
        left_all(y_send.at[v], q[v].at[:, :, pl.ds(0, 384 * WIDTH[v])])
        left_all(d_send.at[v], q[v].at[:, :, pl.ds(0, 2048)])
    left_all(o_send.at[0], shift_row)
    left_all(o_send.at[1], picked.at[pl.ds(0, 6)])
    left_all(o_send.at[2], packed.at[pl.ds(0, 3)])
    left_all(rel_send, relayed)
    left_all(dir_send, near)
    left_all(fwd_send, onward)
    left_all(two_send, second_out)


def per_device(psi, shifts, left_ops, right_ops):
    row = jnp.zeros((8, 128), jnp.int32).at[0, :6].set(shifts)
    dma = pltpu.SemaphoreType.DMA
    some = pl.BlockSpec(memory_space=pl.ANY)
    pairs = [
        (2, 4, 3), (2, 4, 4), (2, 4, 4), (2, 7), (3,),
    ]
    return pl.pallas_call(
        kernel,
        out_shape=jax.ShapeDtypeStruct((2, 512, B), F32),
        in_specs=[pl.BlockSpec(memory_space=pltpu.SMEM), some, some, some, some],
        out_specs=pl.BlockSpec(memory_space=pltpu.VMEM),
        scratch_shapes=[
            pltpu.VMEM((16, QUARTER, 16 * B), BF16),
            pltpu.VMEM((16, QUARTER, 16 * B), BF16),
            pltpu.VMEM((6, 16, B, 128), BF16),
            pltpu.VMEM((12, 4, B, B), BF16),
            pltpu.VMEM((8, 12 * QUARTER, B), BF16),
            pltpu.VMEM((4, 8, B, B), F32),
            pltpu.VMEM((16, B, B), BF16),
            pltpu.VMEM((16, B, B), BF16),
            pltpu.VMEM((2, 8, 128), jnp.int32),
            pltpu.SMEM((2, 8, 128), jnp.int32),
            pltpu.VMEM((2, 2, 4, B, B), BF16),
            pltpu.VMEM((2, 2, 2, 4, 128, B), BF16),
            pltpu.VMEM((2, 2, 2, 4, 128, B), BF16),
            pltpu.VMEM((2, 2, 2, 4, 128, B), BF16),
            pltpu.VMEM((2, 2, 2, 4, B, B), BF16),
            pltpu.VMEM((2, 2, 3, B, B), BF16),
            pltpu.VMEM((2, 2, 3, B, B), BF16),
        ]
        + [dma(shape[:1] if sender else shape) for shape in pairs for sender in (True, False)]
        + [dma((2, 4)), dma((12,)), dma((2,))]
        + [dma, dma((2, 2, 2, 4))] * 3
        + [dma, dma((2, 2, 3))],
        compiler_params=pltpu.CompilerParams(
            collective_id=0, has_side_effects=True, vmem_limit_bytes=62 * MIB
        ),
        name="sigma",
    )(shifts, row, psi, left_ops, right_ops)


def solution(mesh):
    in_specs = (
        P(None, "blocks", None),
        P("terms"),
        P("terms", None, None, None),
        P("terms", None, None, None),
    )
    out_specs = P(None, "terms", "blocks")
    return jax.shard_map(
        per_device, mesh=mesh, in_specs=in_specs, out_specs=out_specs, check_vma=False
    )
```

time: 786 us -> 113 us (0.14)
  waiting for transfers between devices: 550 us -> 0 us
  local copies, waits for them, and re-layouts: 142 us -> 3.51 us
  Pallas kernels: 0 us -> 110 us
  matrix products: 41.3 us -> 0 us
  other arithmetic: 22.8 us -> 0 us
  starting transfers between devices: 13.5 us -> 0 us
  between operations: 13.5 us -> 0.01 us
    all_to_all x2 -> x0, waiting for transfers between devices: 446 us -> none  [per_device(): lax.all_to_all(outgoing, 'blocks', split_axis=3, concat_axis=2, tiled=True)]
    pallas_call x0 -> x1, Pallas kernels: none -> 110 us  [per_device(): pl.pallas_call(kernel, out_shape=jax.ShapeDtypeStruct((2, 512, B), F32),...]
    psum x1 -> x0, waiting for transfers between devices: 105 us -> none  [per_device(): totals = lax.psum(partial_value, 'terms')]
    gather x8 -> x0, local copies, waits for them, and re-layouts: 58.8 us -> none  [the longest x3 23.5 us: second_section(): jnp.take_along_axis(blocked, positions[None, :, :, None, None], axis=2)]
    all_to_all x2 -> x0, local copies, waits for them, and re-layouts: 44.1 us -> none  [per_device(): lax.all_to_all(outgoing, 'blocks', split_axis=3, concat_axis=2, tiled=True)]
    dot_general x4 -> x0, matrix products: 41.3 us -> none  [the longest x2 21.3 us: second_section(): jnp.einsum('tnab,vtnbc->vnac', moved_left, moved_blocks, preferred_elemen...]
    select_n x2 -> x0, local copies, waits for them, and re-layouts: 25.6 us -> none  [first_section(): jnp.take_along_axis(product, positions[None, :, None, :, None], axis=3)]
    select_n x1 -> x0, other arithmetic: 13.7 us -> none  [first_section(): jnp.take_along_axis(product, positions[None, :, None, :, None], axis=3)]
  transfers between devices with their start and end apart: 3 -> 0, of which waited for: 3 -> 0; matrix products, arithmetic and copies ran while one was open for 6% -> 0% of each run, Pallas kernels for 0% -> 0%
where the time goes in v2:
time: 113 us
  Pallas kernels  110 us (97%)
  local copies, waits for them, and re-layouts  3.51 us (3%)
    pallas_call x1, Pallas kernels, per_device(): pl.pallas_call(kernel, out_shape=jax.ShapeDtypeStruct((2, 512, B), F32),...  110 us
    unnamed x1, local copies, waits for them, and re-layouts  2.26 us

profile of v2, /device:TPU:0, one launch (start us, length us, event | category | flops | bytes accessed | tf_op | source)
XLA Modules:
  0.0 113.1 jit_solution(7387122240336393783)
XLA Ops:
  0.0 1.3 %scatter.4.shift_row = s32[8,128]{1,0:T(8,128)} pad(s32[1,6]{1,0:T(1,128)} %bitcast.1, s32[]{:T(128)} %constant.26.clone.1), padding=0_7x0_122 | pad | bytes 4124 | tf_op jit(solution)/shard_map/scatter | solution.py:460
  1.3 109.6 %sigma.1 = f32[2,512,256]{2,1,0:T(8,128)} custom-call(s32[6]{0:T(128)} %shifts.1, s32[8,128]{1,0:T(8,128)} %scatter.4.shift_row, bf16[2,256,4096]{2,1,0:T(8,128)(2,1)} %psi.1, bf16[6,16,256,256]{3,2,1,0:T(8,128)(2,1)} %left.1, bf16[6,16,256,256]{3,2,1,0:T(8,128)(2,1)} %right.1), custom_call_target="tpu_custom_call" | custom-call | tf_op jit(solution)/shard_map/sigma/pallas_call | solution.py:466
  110.9 2.3 %copy.6 = f32[2,512,256]{2,1,0:T(8,128)} copy(f32[2,512,256]{2,1,0:T(8,128)} %sigma.1) | data formatting | bytes 2097152

commit v3 on v2

--- a/solution.py
+++ b/solution.py
@@ -25,7 +25,7 @@
     shifts, shift_row, psi, left, right, out,
     q_first, q_last, packed, picked, moved, held, stage_even, stage_odd, shift_all, shift_words,
     far, near, relayed, onward, first, second_out, second,
-    x_send, x_recv, z_send, z_recv, y_send, y_recv, d_send, d_recv, o_send, o_recv,
+    x_send, x_recv, z_send, z_recv, row_recv, y_send, y_recv, d_send, d_recv, o_send, o_recv,
     local_sem, stage_sem, shift_sem,
     rel_send, rel_recv, dir_send, dir_recv, fwd_send, fwd_recv, two_send, two_recv,
 ):
@@ -84,6 +84,7 @@
     zs = [(z_send.at[v], z_recv) for v in range(2)]
     ys = [(y_send.at[v], y_recv) for v in range(2)]
     ds = [(d_send.at[v], d_recv) for v in range(2)]
+    rs = (z_send.at[0], row_recv)
     os = [(o_send.at[k], o_recv) for k in range(3)]
     base = 2048 * core
     me = 4 * z + x
@@ -140,6 +141,46 @@
         )
         if number == 0:
             y_start(v, 0)
+
+    STEPS = (0, 1, 3, 2)
+
+    def row_of(zz, d, window):
+        return q[0].at[4 * zz + wrap(x + d), :, window]
+
+    def row_send(number, k, source, target):
+        for way, step in ((0, 1), (1, -1)):
+            state["r", number, way, k] = send(
+                source, target, rs, (number, 4 * way + k), on(dz=step)
+            )
+
+    def own_start(number):
+        window = window_of(0, number)
+        source = psi.at[0, pl.ds(pl.multiple_of(QUARTER * x, QUARTER), QUARTER), window]
+        row_send(number, 0, source, row_of(z, 0, window))
+
+    def rows_start(number):
+        copies, own = state["x", 0, number]
+        for copy, k in ((copies[0], 1), (copies[1], 2), (copies[2], 3)):
+            copy.wait_recv()
+            view = row_of(z, -STEPS[k], window_of(0, number))
+            row_send(number, k, view, view)
+        own.wait()
+        if number == 0:
+            y_start(0, 0)
+
+    def row_pass(number, *which):
+        for k in which:
+            way, step = ((0, 1), (1, -1))[k // 2]
+            state["r", number, way, k].wait_recv()
+            view = row_of(groups[1 + way], -STEPS[k], window_of(0, number))
+            state["rr", number, k] = send(view, view, rs, (number, 8 + k), on(dz=step))
+
+    def rows_done(number):
+        for k in range(4):
+            state["r", number, 1 - k // 2, k].wait_recv()
+        if number == 0:
+            y_start(0, 1)
+            y_start(0, 2)
 
     def y_start(v, g):
         view = rows_of(v, groups[g], lanes(v, y))
@@ -164,7 +205,7 @@
         state["zz", v, number] = one, two
 
     def z_done(v, number):
-        for copy in state["zz", v, number]:
+        for copy in state["zz", v, number] if v else [state["rr", number, k] for k in range(4)]:
             copy.wait_recv()
         if number == 0:
             y_start(v, 3)
@@ -185,7 +226,7 @@
         for copy in state["yy", v, g]:
             copy.wait_recv()
         view = rows_of(v, groups[g], all_lanes(v))
-        state["d", v, -g] = send(view, view, ds[v], (v, 3 + g), partner)
+        state["d", v, -g] = send(view, view, ds[v], (v, 4 + g), partner)
 
     def gathered(v):
         for number in range(-3, PIECES[v] + 1):
@@ -391,52 +432,72 @@
         for _ in range(count):
             next(step, None)
 
-    x_start(0)
-    go(ops)
-    z_start(0, 0)
-    z_start(0, 1)
-    go(ops)
-    z_pass(0, 0)
-    z_start(0, 2)
+    for number in range(3):
+        own_start(number)
+        x_part(0, number, window_of(0, number))
+    go(ops)
+    rows_start(0)
+    row_pass(0, 0)
+    go(ops)
+    row_pass(0, 2, 1, 3)
+    rows_done(0)
+    rows_start(1)
+    go(ops)
+    z_done(0, 0)
+    rows_start(2)
+    y_pass(0, 0)
+    row_pass(1, 0)
+    row_pass(2, 0)
     x_start(1)
-    go(ops, 2)
-    z_done(0, 0)
-    y_pass(0, 0)
+    go(ops)
     y_pass(0, 1)
     y_pass(0, 2)
-    go(ops, 2)
-    z_pass(0, 1)
+    row_pass(1, 2, 1, 3)
+    go(ops)
     y_pass(0, 3)
-    z_pass(0, 2)
-    go(ops, 2)
-    for number in range(4):
-        z_start(1, number)
+    row_pass(2, 2, 1, 3)
+    z_start(1, 0)
+    go(ops)
     for g in range(4):
         y_done(0, g)
+    for number in range(1, 4):
+        z_start(1, number)
+    go(ops)
+    rows_done(1)
     z_done(0, 1)
+    rows_done(2)
     z_done(0, 2)
     go(ops, 9)
     gathered(0)
     first_sum = reduce(0)
-    go(first_sum)
+    go(first_sum, 2)
     z_pass(1, 0)
-    go(first_sum)
+    go(first_sum, 2)
     z_done(1, 0)
-    go(first_sum)
-    for number in range(1, 4):
-        z_pass(1, number)
-    go(first_sum)
-    for g in range(4):
-        y_pass(1, g)
-    go(first_sum)
+    go(first_sum, 2)
+    z_pass(1, 1)
+    y_pass(1, 0)
+    y_pass(1, 1)
+    y_pass(1, 2)
+    go(first_sum, 2)
+    z_pass(1, 2)
+    z_pass(1, 3)
+    go(first_sum, 2)
+    y_pass(1, 3)
+    go(first_sum, 2)
     for number in range(1, 4):
         z_done(1, number)
-    go(first_sum)
     for g in range(4):
         y_done(1, g)
-    go(first_sum, 100)
     gathered(1)
-    go(reduce(1), 100)
+    second_sum = reduce(1)
+    go(second_sum, 2)
+    go(first_sum, 2)
+    go(second_sum, 2)
+    go(first_sum, 2)
+    go(second_sum, 2)
+    go(first_sum, 9)
+    go(second_sum, 100)
 
     def left_all(semaphore, ref):
         pltpu.make_async_copy(ref, ref, semaphore).wait()
@@ -460,9 +521,6 @@
     row = jnp.zeros((8, 128), jnp.int32).at[0, :6].set(shifts)
     dma = pltpu.SemaphoreType.DMA
     some = pl.BlockSpec(memory_space=pl.ANY)
-    pairs = [
-        (2, 4, 3), (2, 4, 4), (2, 4, 4), (2, 7), (3,),
-    ]
     return pl.pallas_call(
         kernel,
         out_shape=jax.ShapeDtypeStruct((2, 512, B), F32),
@@ -487,8 +545,9 @@
             pltpu.VMEM((2, 2, 3, B, B), BF16),
             pltpu.VMEM((2, 2, 3, B, B), BF16),
         ]
-        + [dma(shape[:1] if sender else shape) for shape in pairs for sender in (True, False)]
-        + [dma((2, 4)), dma((12,)), dma((2,))]
+        + [dma((2,)), dma((2, 5, 3)), dma((2,)), dma((2, 4, 4)), dma((4, 12)), dma((2,)), dma((2, 4, 4))]
+        + [dma((2,)), dma((2, 8)), dma((3,)), dma((3,))]
+        + [dma((2, 5)), dma((12,)), dma((2,))]
         + [dma, dma((2, 2, 2, 4))] * 3
         + [dma, dma((2, 2, 3))],
         compiler_params=pltpu.CompilerParams(

time: 113 us -> 108 us (0.956)
  Pallas kernels: 110 us -> 104 us
    pallas_call x1, Pallas kernels: 110 us -> 104 us  [per_device(): pl.pallas_call(kernel, out_shape=jax.ShapeDtypeStruct((2, 512, B), F32),...]
where the time goes in v3:
time: 108 us
  Pallas kernels  104 us (96%)
  local copies, waits for them, and re-layouts  3.51 us (3%)
    pallas_call x1, Pallas kernels, per_device(): pl.pallas_call(kernel, out_shape=jax.ShapeDtypeStruct((2, 512, B), F32),...  104 us
    unnamed x1, local copies, waits for them, and re-layouts  2.26 us

profile of v3, /device:TPU:0, one launch (start us, length us, event | category | flops | bytes accessed | tf_op | source)
XLA Modules:
  0.0 108.0 jit_solution(14499065708487302917)
XLA Ops:
  0.0 1.3 %scatter.4.shift_row = s32[8,128]{1,0:T(8,128)} pad(s32[1,6]{1,0:T(1,128)} %bitcast.1, s32[]{:T(128)} %constant.26.clone.1), padding=0_7x0_122 | pad | bytes 4124 | tf_op jit(solution)/shard_map/scatter | solution.py:521
  1.3 104.4 %sigma.1 = f32[2,512,256]{2,1,0:T(8,128)} custom-call(s32[6]{0:T(128)} %shifts.1, s32[8,128]{1,0:T(8,128)} %scatter.4.shift_row, bf16[2,256,4096]{2,1,0:T(8,128)(2,1)} %psi.1, bf16[6,16,256,256]{3,2,1,0:T(8,128)(2,1)} %left.1, bf16[6,16,256,256]{3,2,1,0:T(8,128)(2,1)} %right.1), custom_call_target="tpu_custom_call" | custom-call | tf_op jit(solution)/shard_map/sigma/pallas_call | solution.py:524
  105.7 2.3 %copy.6 = f32[2,512,256]{2,1,0:T(8,128)} copy(f32[2,512,256]{2,1,0:T(8,128)} %sigma.1) | data formatting | bytes 2097152

commit v4 on v3

--- a/solution.py
+++ b/solution.py
@@ -85,7 +85,7 @@
     ys = [(y_send.at[v], y_recv) for v in range(2)]
     ds = [(d_send.at[v], d_recv) for v in range(2)]
     rs = (z_send.at[0], row_recv)
-    os = [(o_send.at[k], o_recv) for k in range(3)]
+    os = [(o_send.at[k], o_recv) for k in range(5)]
     base = 2048 * core
     me = 4 * z + x
 
@@ -248,6 +248,7 @@
             if term % 2 == 1:
                 yield
         swap_right = send(picked.at[pl.ds(0, 6)], picked.at[pl.ds(6, 6)], os[1], 1, partner)
+        swap_left = []
         for pair in range(3):
             slot = pair % 2
             for copy in loads[6 + pair]:
@@ -264,8 +265,11 @@
                 lax.fori_loop(8 * part, 8 * part + 8, pack, 0, unroll=2)
                 if part == 1 and pair == 0:
                     loads[8] = fill_left(2)
+                if part == 1:
+                    swap_left.append(
+                        send(packed.at[pair], packed.at[3 + pair], os[2 + pair], 2 + pair, partner)
+                    )
                 yield
-        swap_left = send(packed.at[pl.ds(0, 3)], packed.at[pl.ds(3, 3)], os[2], 2, partner)
         row_copy.wait()
         swap_row.wait_recv()
         words = pltpu.make_async_copy(shift_all, shift_words, shift_sem.at[1])
@@ -273,7 +277,8 @@
         words.wait()
         yield
         swap_right.wait_recv()
-        swap_left.wait_recv()
+        for swap in swap_left:
+            swap.wait_recv()
 
     def column(v, turn):
         member = wrap(x + OFFSETS[turn])
@@ -462,7 +467,7 @@
         y_done(0, g)
     for number in range(1, 4):
         z_start(1, number)
-    go(ops)
+    go(ops, 4)
     rows_done(1)
     z_done(0, 1)
     rows_done(2)
@@ -510,7 +515,8 @@
         left_all(d_send.at[v], q[v].at[:, :, pl.ds(0, 2048)])
     left_all(o_send.at[0], shift_row)
     left_all(o_send.at[1], picked.at[pl.ds(0, 6)])
-    left_all(o_send.at[2], packed.at[pl.ds(0, 3)])
+    for pair in range(3):
+        left_all(o_send.at[2 + pair], packed.at[pair])
     left_all(rel_send, relayed)
     left_all(dir_send, near)
     left_all(fwd_send, onward)
@@ -546,7 +552,7 @@
             pltpu.VMEM((2, 2, 3, B, B), BF16),
         ]
         + [dma((2,)), dma((2, 5, 3)), dma((2,)), dma((2, 4, 4)), dma((4, 12)), dma((2,)), dma((2, 4, 4))]
-        + [dma((2,)), dma((2, 8)), dma((3,)), dma((3,))]
+        + [dma((2,)), dma((2, 8)), dma((5,)), dma((5,))]
         + [dma((2, 5)), dma((12,)), dma((2,))]
         + [dma, dma((2, 2, 2, 4))] * 3
         + [dma, dma((2, 2, 3))],

time: 108 us -> 107 us (level)
    pallas_call x1, Pallas kernels: 104 us -> 103 us  [per_device(): pl.pallas_call(kernel, out_shape=jax.ShapeDtypeStruct((2, 512, B), F32),...]
where the time goes in v4:
time: 107 us; the launch traced here: 106 us
  Pallas kernels  103 us (96%)
  local copies, waits for them, and re-layouts  3.51 us (3%)
    pallas_call x1, Pallas kernels, per_device(): pl.pallas_call(kernel, out_shape=jax.ShapeDtypeStruct((2, 512, B), F32),...  103 us
    unnamed x1, local copies, waits for them, and re-layouts  2.26 us

profile of v4, /device:TPU:0, one launch (start us, length us, event | category | flops | bytes accessed | tf_op | source)
XLA Modules:
  0.0 106.5 jit_solution(13734562193396479875)
XLA Ops:
  0.0 1.3 %scatter.4.shift_row = s32[8,128]{1,0:T(8,128)} pad(s32[1,6]{1,0:T(1,128)} %bitcast.1, s32[]{:T(128)} %constant.26.clone.1), padding=0_7x0_122 | pad | bytes 4124 | tf_op jit(solution)/shard_map/scatter | solution.py:527
  1.3 103.0 %sigma.1 = f32[2,512,256]{2,1,0:T(8,128)} custom-call(s32[6]{0:T(128)} %shifts.1, s32[8,128]{1,0:T(8,128)} %scatter.4.shift_row, bf16[2,256,4096]{2,1,0:T(8,128)(2,1)} %psi.1, bf16[6,16,256,256]{3,2,1,0:T(8,128)(2,1)} %left.1, bf16[6,16,256,256]{3,2,1,0:T(8,128)(2,1)} %right.1), custom_call_target="tpu_custom_call" | custom-call | tf_op jit(solution)/shard_map/sigma/pallas_call | solution.py:530
  104.2 2.3 %copy.6 = f32[2,512,256]{2,1,0:T(8,128)} copy(f32[2,512,256]{2,1,0:T(8,128)} %sigma.1) | data formatting | bytes 2097152
